TPU v7x, 32 devices: a whole 2x2x4 slice. The times are simulated.
32 devices in a mesh: wide: 16 (over z, y, x), narrow: 2 (over core).
Axes of the slice: x: 2, y: 2, z: 4, core: 2. Of those that a mesh axis runs over, the one named last changes fastest.
Arguments:
- residual: bfloat16 [64, 16384], P('narrow', 'wide'), may hold values from -54 to 54
- norm_gain: bfloat16 [16384], P('wide'), may hold values from 0.5 to 1.5
- w_query: bfloat16 [16384, 16384], P('wide', 'narrow'), may hold values from -0.046875 to 0.046875
- w_keyval: bfloat16 [16384, 2, 1024], P('wide', None, 'narrow'), may hold values from -0.046875 to 0.046875
- w_out: bfloat16 [16384, 16384], P('narrow', 'wide'), may hold values from -0.375 to 0.375
- cache_rows: bfloat16 [64, 768, 2, 1024], P('wide', None, None, 'narrow'), may hold values from -106 to 106, as said below
- lengths: int32 [64], replicated, may hold values from 1 to 768, 12288 in all
- assignment: int32 [64], replicated, may hold values from 0 to 63, each once
Outputs:
- layer_out: bfloat16 [64, 16384], P('narrow', 'wide')
Inputs may be any that keep to these rules, and one draw needn't show every extreme that they name: `lengths`: largest entry reaches 768. `assignment`: each row named once. `cache_rows`: entries at positions at or beyond a row's length are not read.
All inputs are finite; a program needn't handle non-finite values.
Results may differ from a plain program's by a relative error of at most 0.012.
The roundings to bfloat16 on the way count: a program that leaves them out, or rounds other values in their place, can miss the bound.
Values may be sent and summed in bfloat16 or wider, within the bound.
No kernel may reach another device: no remote copies, remote signals or barrier semaphores. Data moves between devices by JAX's collectives and lax.ppermute only.
A program may use at most 128 MiB of HBM per device.

v0:
```python
import math

import jax
import jax.numpy as jnp
from jax import lax
from jax.sharding import PartitionSpec as P

D = 16384
HD = 128


def rotate(values, positions):
    half_dim = values.shape[-1] // 2
    freqs = 500000.0 ** (-(jnp.arange(half_dim, dtype=jnp.float32) * 2.0 / values.shape[-1]))
    angles = positions[..., None] * freqs
    cosine = jnp.cos(angles)
    sine = jnp.sin(angles)
    first_half = values[..., :half_dim]
    second_half = values[..., half_dim:]
    return jnp.concatenate(
        [first_half * cosine - second_half * sine, second_half * cosine + first_half * sine],
        axis=-1,
    )


def attend(queries, keys_new, values_new, cache_rows, slot_lengths, block_count, block_len):
    slot_count, groups_local, group_size, head_dim = queries.shape
    scale = 1.0 / math.sqrt(head_dim)
    own_score = (
        jnp.einsum("skgd,skd->skg", queries, keys_new, preferred_element_type=jnp.float32) * scale
    )

    def block_scores(number):
        offset = number * block_len
        stored = lax.dynamic_slice_in_dim(cache_rows, offset, block_len, 1)
        keys = stored[:, :, 0].reshape(slot_count, block_len, groups_local, head_dim)
        values = stored[:, :, 1].reshape(slot_count, block_len, groups_local, head_dim)
        scores = (
            jnp.einsum("skgd,sjkd->skgj", queries, keys, preferred_element_type=jnp.float32) * scale
        )
        live_mask = (offset + jnp.arange(block_len, dtype=jnp.int32))[None, :] < slot_lengths[
            :, None
        ]
        scores = jnp.where(live_mask[:, None, None, :], scores, -jnp.inf)
        return (scores, values)

    def first_pass(number, running):
        maxima, totals = running
        scores, unused = block_scores(number)
        new_max = jnp.maximum(maxima, jnp.max(scores, axis=-1))
        totals = totals * jnp.exp(maxima - new_max) + jnp.sum(
            jnp.exp(scores - new_max[..., None]), axis=-1
        )
        return (new_max, totals)

    maxima, totals = lax.fori_loop(
        0, block_count, first_pass, (own_score, jnp.ones_like(own_score))
    )
    own_prob = (jnp.exp(own_score - maxima) / totals).astype(jnp.bfloat16)
    start_sum = (
        own_prob.astype(jnp.float32)[..., None] * values_new.astype(jnp.float32)[:, :, None, :]
    )

    def second_pass(number, summed):
        scores, values = block_scores(number)
        probs = (jnp.exp(scores - maxima[..., None]) / totals[..., None]).astype(jnp.bfloat16)
        return summed + jnp.einsum(
            "skgj,sjkd->skgd", probs, values, preferred_element_type=jnp.float32
        )

    return lax.fori_loop(0, block_count, second_pass, start_sum)


def per_device(residual, norm_gain, w_query, w_keyval, w_out, cache_rows, lengths, assignment):
    slot_count = cache_rows.shape[0]
    most_len = cache_rows.shape[1]
    channels = cache_rows.shape[3]
    query_cols = w_query.shape[1]
    width_local = w_query.shape[0]
    groups_local = channels // HD
    group_size = query_cols // channels
    row_count = slot_count * lax.axis_size("wide")
    inputs = residual.astype(jnp.float32)
    gain_local = norm_gain.astype(jnp.float32)
    gathered = lax.all_gather(residual, "narrow", axis=0, tiled=True).astype(jnp.float32)
    squares = lax.psum(jnp.sum(gathered * gathered, axis=1), "wide")
    inverse_rms = lax.rsqrt(squares / D + 1e-05)
    normed = (gathered * inverse_rms[:, None] * gain_local[None, :]).astype(jnp.bfloat16)
    slot_rows = normed[assignment]
    keyval_flat = w_keyval.reshape(width_local, 2 * channels)
    combined = lax.psum_scatter(
        jnp.concatenate(
            [
                jnp.dot(slot_rows, w_query, preferred_element_type=jnp.float32),
                jnp.dot(slot_rows, keyval_flat, preferred_element_type=jnp.float32),
            ],
            axis=1,
        ),
        "wide",
        scatter_dimension=0,
        tiled=True,
    )
    query_raw = combined[:, :query_cols]
    keyval_raw = combined[:, query_cols:]
    owned_rows = lax.dynamic_slice_in_dim(
        assignment, lax.axis_index("wide") * slot_count, slot_count
    )
    slot_lengths = lengths[owned_rows]
    positions = slot_lengths.astype(jnp.float32)[:, None]
    queries = rotate(query_raw.reshape(slot_count, query_cols // HD, HD), positions).astype(
        jnp.bfloat16
    )
    queries = queries.reshape(slot_count, groups_local, group_size, HD)
    keyval_heads = keyval_raw.reshape(slot_count, 2, groups_local, HD)
    keys_new = rotate(keyval_heads[:, 0], positions).astype(jnp.bfloat16)
    values_new = keyval_heads[:, 1].astype(jnp.bfloat16)
    block_len = min(128, most_len)
    block_count = most_len // block_len
    attended = attend(
        queries, keys_new, values_new, cache_rows, slot_lengths, block_count, block_len
    )
    attended = attended.reshape(slot_count, query_cols).astype(jnp.bfloat16)
    slot_update = jnp.dot(
        lax.all_gather(attended, "wide", axis=0, tiled=True),
        w_out,
        preferred_element_type=jnp.float32,
    )
    slot_of = (
        jnp.zeros((row_count,), jnp.int32)
        .at[assignment]
        .set(jnp.arange(row_count, dtype=jnp.int32))
    )
    row_update = slot_update[slot_of]
    update = lax.psum_scatter(row_update, "narrow", scatter_dimension=0, tiled=True)
    return (inputs + update).astype(jnp.bfloat16)


def solution(mesh):
    placed = (
        P("narrow", "wide"),
        P("wide"),
        P("wide", "narrow"),
        P("wide", None, "narrow"),
        P("narrow", "wide"),
        P("wide", None, None, "narrow"),
        P(),
        P(),
    )
    return jax.shard_map(
        per_device, mesh=mesh, in_specs=placed, out_specs=P("narrow", "wide"), check_vma=False
    )
```

profile of v0, /device:TPU:0, one launch (start us, length us, event | category | flops | bytes accessed | tf_op | source)
XLA Modules:
  0.0 301.4 jit_solution(3782112785006373354)
XLA Ops:
  6.5 2.3 all_gather.6
  9.0 43.4 %psum.7 = f32[64]{0:T(128)S(1)} all-reduce(f32[64]{0:T(128)S(1)} %fusion.15), channel_id=1, replica_groups=mesh['wide'=16,'narrow'=2] {'wide'}, use_global_device_ids=true, to_apply=%region_1.0 | all-reduce | flops 64 | bytes 512 | tf_op jit(solution)/shard_map/psum | solution.py:86
  52.4 0.7 convert_element_type.62
  53.7 2.1 copy.23
  56.0 0.7 gather_fusion
  57.2 8.8 %fusion.27 = f32[64,8192]{1,0:T(8,128)S(1)} fusion(bf16[64,1024]{1,0:T(8,128)(2,1)S(1)} %gather_fusion, bf16[1024,8192]{1,0:T(8,128)(2,1)} %param.14), kind=kOutput, calls=%fused_computation.70 | convolution fusion | flops 1073741824 | bytes 19005440 | tf_op jit(solution)/shard_map/dot_general | solution.py:94
  66.0 1.6 pad_maximum_fusion
  69.0 16.2 %copy.16 = bf16[4,768,2,512]{1,3,0,2:T(8,128)(2,1)} copy(bf16[4,768,2,512]{3,2,1,0:T(2,128)(2,1)} %param.17) | data formatting | bytes 12582912
  86.6 108.1 %all-reduce.3.cloned.1.call-done = f32[64,9216]{1,0:T(8,128)} async-done(((f32[64,9216]{1,0:T(8,128)}), f32[64,9216]{1,0:T(8,128)}) %all-reduce.3.cloned.1.call-update) | async-done | bytes 2359312
  194.7 0.8 dynamic-slice.6
  195.6 1.0 dynamic-slice_bitcast_fusion
  197.1 10.8 %while.30 = (s32[]{:T(128)}, f32[4,4,16]{2,1,0:T(4,128)S(1)}, f32[4,4,16]{2,1,0:T(4,128)S(1)}, s32[4]{0:T(128)S(1)}, bf16[4,768,2,512]{1,3,0,2:T(8,128)(2,1)}, /...) while((s32[]{:T(128)}, f32[4,4,16]{2,1,0:T(4,128)S(1)}, ...), condition=%wide.region_6.7_spmd.clone, body=%wide.region_3.6_spmd.clone.sunk | while | flops 8553863 | bytes 1916085 | solution.py:56
  197.2 1.1 constant_dynamic-slice_fusion.6
  198.9 1.1 constant_dynamic-slice_fusion.6
  200.7 1.1 constant_dynamic-slice_fusion.6
  202.5 1.1 constant_dynamic-slice_fusion.6
  204.3 1.1 constant_dynamic-slice_fusion.6
  206.1 1.1 constant_dynamic-slice_fusion.6
  208.0 11.5 %while.29 = (s32[]{:T(128)}, f32[4,4,16,128]{3,2,1,0:T(8,128)S(1)}, s32[4]{0:T(128)S(1)}, bf16[4,768,2,512]{1,3,0,2:T(8,128)(2,1)}, bf16[4,4,16,128]{3,2,1,0:T(8...) while((s32[]{:T(128)}, f32[4,4,16,128]{3,2,1,0:T(8,128)S(1)}, ...), condition=%wide.region_8.9_spmd, body=%wide.region_7.8_spmd.sunk | while | flops 16974472 | bytes 3477707 | solution.py:71
  208.1 1.3 constant_dynamic-slice_fusion.5
  210.0 1.3 constant_dynamic-slice_fusion.5
  211.9 1.3 constant_dynamic-slice_fusion.5
  213.8 1.3 constant_dynamic-slice_fusion.5
  215.7 1.3 constant_dynamic-slice_fusion.5
  217.6 1.3 constant_dynamic-slice_fusion.5
  220.3 0.8 scatter_custom_fusion
  221.1 54.1 %all-gather.3.cloned.1.call-done = bf16[16,4,8192]{2,1,0:T(4,128)(2,1)} async-done(((bf16[1,4,8192]{2,1,0:T(4,128)(2,1)}), bf16[16,4,8192]{2,1,0:T(4,128)(2,1)}) %all-gather.3.cloned.1.call-update) | async-done | bytes 1048592 | tf_op jit(solution)/shard_map/all_gather | solution.py:124
  275.2 1.3 reshape.197
  276.5 8.8 %fusion.29 = f32[64,1024]{1,0:T(8,128)S(1)} fusion(bf16[64,8192]{1,0:T(8,128)(2,1)S(1)} %reshape.197, bf16[8192,1024]{1,0:T(8,128)(2,1)} %param.16), kind=kOutput, calls=%fused_computation.72 | convolution fusion | flops 1073741824 | bytes 18087936 | tf_op jit(solution)/shard_map/dot_general | solution.py:123
  285.4 1.4 gather_fusion.2
  286.7 6.6 %reduce-scatter.2.cloned.1.call-done = f32[32,1024]{1,0:T(8,128)} async-done(((f32[64,1024]{1,0:T(8,128)}), f32[32,1024]{1,0:T(8,128)}) %reduce-scatter.2.cloned.1.call-update) | async-done | bytes 131088 | tf_op jit(solution)/shard_map/reduce_scatter | solution.py:134
  293.4 1.5 add_convert_fusion
  (105 shorter events, 12.4 us)
Async XLA Ops:
  6.5 61.8 %copy-start = (s32[64]{0:T(128)S(1)}, s32[64]{0:T(128)}, u32[]{:S(2)}) copy-start(s32[64]{0:T(128)} %param.18) | copy-start | bytes 772
  6.5 188.2 %all-reduce.3.cloned.1.call-start = ((), (), s32[]{:S(2)}) async-start(), calls=%async_computation.3 | async-start | bytes 4718592
  67.6 0.7 copy-start.2
  67.7 207.5 %all-gather.3.cloned.1.call-start = ((), (), s32[]{:S(2)}) async-start(), calls=%async_computation.2 | async-start | bytes 1114112 | tf_op jit(solution)/shard_map/all_gather | solution.py:124
  69.0 16.2 %copy-start.3 = (u32[32]{0:T(128)S(1)}, u32[32]{0:T(128)}, u32[]{:S(2)}) copy-start(u32[32]{0:T(128)} %constant.123) | copy-start | bytes 388
  220.2 73.1 %reduce-scatter.2.cloned.1.call-start = ((), (), s32[]{:S(2)}) async-start(), calls=%async_computation.1 | async-start | bytes 393216 | tf_op jit(solution)/shard_map/reduce_scatter | solution.py:134
  285.3 8.0 %copy-start.1 = (bf16[32,1024]{1,0:T(8,128)(2,1)S(1)}, bf16[32,1024]{1,0:T(8,128)(2,1)}, u32[]{:S(2)}) copy-start(bf16[32,1024]{1,0:T(8,128)(2,1)} %param.12) | copy-start | bytes 196612
Sparse Core Ops, SparseCore 0:
  67.8 126.9 all-reduce.2
  220.4 54.7 all-gather.2
  286.9 6.4 reduce-scatter.1
where the time goes:
time: 303 us; the launch traced here: 301 us
  waiting for transfers between devices  169 us (56%)
  blocking collectives  45.7 us (15%)
  local copies, waits for them, and re-layouts  41.2 us (14%)
  matrix products  23.3 us (8%)
  between operations  14 us (5%)
  other arithmetic  7.9 us (3%)
    unnamed x4, waiting for transfers between devices  108 us
    all_gather x1, waiting for transfers between devices, per_device(): lax.all_gather(attended, 'wide', axis=0, tiled=True)  54.1 us
    psum x1, blocking collectives, per_device(): squares = lax.psum(jnp.sum(gathered * gathered, axis=1), 'wide')  43.4 us
    unnamed x15, local copies, waits for them, and re-layouts  22.5 us
    slice x12, local copies, waits for them, and re-layouts, block_scores(): stored[:, :, 0].reshape(slot_count, block_len, groups_local, head_dim)  14.3 us
    dot_general x1, matrix products, per_device(): jnp.dot(lax.all_gather(attended, 'wide', axis=0, tiled=True), w_out, pref...  8.82 us
    dot_general x1, matrix products, per_device(): jnp.dot(slot_rows, w_query, preferred_element_type=jnp.float32)  8.8 us
    reduce_scatter x1, waiting for transfers between devices, per_device(): lax.psum_scatter(row_update, 'narrow', scatter_dimension=0, tiled=True)  6.62 us
  transfers between devices with their start and end apart: 3, of which 3 were waited for; matrix products, arithmetic and copies ran while one was open for 6% of the time, Pallas kernels for 0%

commit v1 on v0

v1 whole, which is shorter than its diff:
```python
import functools
import math

import jax
import jax.numpy as jnp
from jax import lax
from jax.experimental import pallas as pl
from jax.experimental.pallas import tpu as pltpu
from jax.sharding import PartitionSpec as P

HD = 128
BF = jnp.bfloat16
F32 = jnp.float32
VMEM_LIMIT = 48 * 1024 * 1024
NT = (((1,), (1,)), ((), ()))


def params(**kw):
    return pltpu.CompilerParams(vmem_limit_bytes=VMEM_LIMIT, **kw)


def log2(n):
    return n.bit_length() - 1


def split_hi_lo(value):
    hi = value.astype(BF)
    return hi, (value - hi.astype(F32)).astype(BF)


def slot_of_row(rel, me, slots, order):
    block = lax.shift_right_logical(rel, log2(slots))
    count = len(order)
    mask = jnp.zeros_like(rel)
    for k, bit in enumerate(order):
        on = lax.bitwise_and(lax.shift_right_logical(rel, log2(slots) + count - 1 - k), 1)
        mask = mask + on * bit
    del block
    return lax.bitwise_xor(mask, me) * slots + lax.bitwise_and(rel, slots - 1)


def one_hot(condition):
    return jnp.where(condition, 1.0, 0.0).astype(BF)


def project_kernel(me_ref, assign_ref, x_ref, gain_ref, w_ref, *rest, slots, order, with_kv):
    if with_kv:
        wkv_ref, keep_ref, send_ref, keep2_ref, send2_ref, lhs = rest
    else:
        keep_ref, send_ref, lhs = rest
    rows = x_ref.shape[0]
    half = rows // 2

    @pl.when(pl.program_id(0) == 0)
    def _():
        rel = lax.broadcasted_iota(jnp.int32, (rows, rows), 0)
        col = lax.broadcasted_iota(jnp.int32, (rows, rows), 1)
        pick = one_hot(slot_of_row(rel, me_ref[0], slots, order) == col)
        named = one_hot(rel == assign_ref[...])
        perm = lax.dot_general(pick, named, NT, preferred_element_type=F32).astype(BF)
        mine = jnp.dot(perm, x_ref[...], preferred_element_type=F32)
        scaled = mine * gain_ref[...].astype(F32)
        hi, lo = split_hi_lo(scaled)
        lhs[:rows, :] = hi
        lhs[rows:, :] = lo
        if with_kv:
            kv = wkv_ref.shape[1]
            both = jnp.dot(lhs[...], wkv_ref[...], preferred_element_type=F32)
            both = both[:rows] + both[rows:]
            keep2_ref[:, :kv] = both[:half]
            send2_ref[:, :kv] = both[half:].astype(BF)
            squares = jnp.sum(mine * mine, axis=1, keepdims=True)
            wide = jnp.broadcast_to(squares, (rows, HD))
            keep2_ref[:, kv : kv + HD] = wide[:half]
            hi, lo = split_hi_lo(wide[half:])
            send2_ref[:, kv : kv + HD] = hi
            send2_ref[:, kv + HD :] = lo

    both = jnp.dot(lhs[...], w_ref[...], preferred_element_type=F32)
    both = both[:rows] + both[rows:]
    keep_ref[...] = both[:half]
    send_ref[...] = both[half:].astype(BF)


def project(me, assignment, x, gain, w, piece, pieces, slots, order, wkv=None):
    rows, depth = x.shape
    cols = w.shape[1] // pieces
    tile = min(1024, cols)
    steps = cols // tile
    half = rows // 2
    whole = lambda a: pl.BlockSpec(a.shape, lambda i: (0,) * a.ndim)
    ins = [me, assignment, x, gain, w]
    in_specs = [
        pl.BlockSpec(memory_space=pltpu.SMEM),
        whole(assignment),
        whole(x),
        whole(gain),
        pl.BlockSpec((depth, tile), lambda i: (0, piece * steps + i)),
    ]
    shapes = [jax.ShapeDtypeStruct((half, cols), F32), jax.ShapeDtypeStruct((half, cols), BF)]
    out_specs = [
        pl.BlockSpec((half, tile), lambda i: (0, i)),
        pl.BlockSpec((half, tile), lambda i: (0, i)),
    ]
    if wkv is not None:
        ins.append(wkv)
        in_specs.append(whole(wkv))
        extra = [
            jax.ShapeDtypeStruct((half, wkv.shape[1] + HD), F32),
            jax.ShapeDtypeStruct((half, wkv.shape[1] + 2 * HD), BF),
        ]
        shapes += extra
        out_specs += [whole(a) for a in extra]
    return pl.pallas_call(
        functools.partial(project_kernel, slots=slots, order=order, with_kv=wkv is not None),
        grid=(steps,),
        in_specs=in_specs,
        out_specs=out_specs,
        out_shape=shapes,
        scratch_shapes=[pltpu.VMEM((2 * rows, depth), BF)],
        compiler_params=params(),
        cost_estimate=pl.CostEstimate(
            flops=4 * rows * depth * cols, bytes_accessed=2 * depth * cols, transcendentals=0
        ),
    )(*ins)


def add_kernel(keep_ref, recv_ref, *outs, parts, squares):
    cols = keep_ref.shape[1] - (HD if squares else 0)
    rows = keep_ref.shape[0] // parts
    total = keep_ref[:, :cols] + recv_ref[:, :cols].astype(F32)
    if squares:
        sq = keep_ref[:, cols:] + (
            recv_ref[:, cols : cols + HD].astype(F32) + recv_ref[:, cols + HD :].astype(F32)
        )
    for part in range(parts):
        here = slice(part * rows, (part + 1) * rows)
        out = outs[part]
        out[:, :cols] = total[here].astype(out.dtype)
        if squares:
            if part == 0:
                out[:, cols:] = sq[here]
            else:
                hi, lo = split_hi_lo(sq[here])
                out[:, cols : cols + HD] = hi
                out[:, cols + HD :] = lo


def add_split(keep, recv, parts, squares):
    rows = keep.shape[0] // parts
    shapes = [jax.ShapeDtypeStruct((rows, keep.shape[1]), F32)]
    shapes += [jax.ShapeDtypeStruct((rows, recv.shape[1]), BF)] * (parts - 1)
    return pl.pallas_call(
        functools.partial(add_kernel, parts=parts, squares=squares),
        out_shape=shapes,
        in_specs=[pl.BlockSpec(memory_space=pltpu.VMEM)] * 2,
        out_specs=[pl.BlockSpec(memory_space=pltpu.VMEM)] * parts,
        compiler_params=params(),
    )(keep, recv)


def exchange(value, axis, bit):
    n = lax.axis_size(axis)
    return lax.ppermute(value, axis, [(i, i ^ bit) for i in range(n)])


def direct_masks(order):
    return [order[-1], order[-2], order[-1] | order[-2]]


def attend_kernel(
    me_ref, lengths_ref, assign_ref, cos_ref, sin_ref, gathered, k_ref, v_ref, out_ref,
    raw, queries, kv_new, result, *, slots, groups, group_size, pieces, width, kv_cols,
):
    step = pl.program_id(0)
    heads = groups * group_size
    head_cols = heads * HD // pieces
    scale = 1.0 / math.sqrt(HD)

    @pl.when(step == 0)
    def _():
        for p in range(pieces):
            keep, *parts = gathered[p]
            total = keep[...]
            for part in parts:
                total = total + part[...].astype(F32)
            for h in range(heads // pieces):
                raw[pl.ds((p * (heads // pieces) + h) * 8, slots), :] = total[
                    :, h * HD : (h + 1) * HD
                ]
        keep, *parts = gathered[pieces]
        total = keep[:, :kv_cols]
        squares = keep[:, kv_cols:]
        for part in parts:
            total = total + part[:, :kv_cols].astype(F32)
            squares = squares + (
                part[:, kv_cols : kv_cols + HD].astype(F32) + part[:, kv_cols + HD :].astype(F32)
            )
        inverse = lax.rsqrt(squares / width + 1e-05)
        for h in range(2 * groups):
            kv_new[h] = total[:, h * HD : (h + 1) * HD] * inverse
        kv_new[2 * groups] = inverse

    def pick(value):
        return value

    length = lengths_ref[assign_ref[me_ref[0] * slots + step]]
    cosine = cos_ref[pl.ds(step, 1), :]
    sine = sin_ref[pl.ds(step, 1), :]
    inverse = kv_new[2 * groups, pl.ds(step, 1), :]
    most = k_ref.shape[2]
    live = lax.broadcasted_iota(jnp.int32, (group_size, most), 1) < length

    def rotate(value):
        return value * cosine + pltpu.roll(value, HD // 2, 1) * sine

    for g in range(groups):
        here = slice(g * HD, (g + 1) * HD)
        query = raw[pl.ds(g * group_size * 8 + step, group_size, stride=8), :] * inverse
        query = rotate(query).astype(BF)
        k_new = rotate(kv_new[g, pl.ds(step, 1), :]).astype(BF).astype(F32)
        v_new = kv_new[groups + g, pl.ds(step, 1), :].astype(BF).astype(F32)
        own = jnp.sum(query.astype(F32) * k_new, axis=1, keepdims=True) * scale
        scores = (
            lax.dot_general(query, k_ref[0, 0, :, here], NT, preferred_element_type=F32) * scale
        )
        scores = jnp.where(live, scores, -jnp.inf)
        top = jnp.maximum(jnp.max(scores, axis=1, keepdims=True), own)
        weights = jnp.exp(scores - top)
        own = jnp.exp(own - top)
        total = jnp.sum(weights, axis=1, keepdims=True) + own
        probs = (weights / total).astype(BF)
        own = (own / total).astype(BF).astype(F32)
        summed = jnp.dot(probs, v_ref[0, 0, :, here], preferred_element_type=F32) + own * v_new
        result[pl.ds(g * group_size * 8 + step, group_size, stride=8), :] = summed

    @pl.when(step == slots - 1)
    def _():
        for p in range(pieces):
            for h in range(heads // pieces):
                out_ref[p][:, h * HD : (h + 1) * HD] = result[
                    pl.ds((p * (heads // pieces) + h) * 8, slots), :
                ].astype(BF)
    del queries, head_cols, pick


def attend(me, lengths, assignment, cosine, sine, gathered, cache, slots, groups, heads, width):
    pieces = len(gathered) - 1
    most, channels = cache.shape[2], cache.shape[3]
    counts = [len(g) for g in gathered]
    flat = [a for g in gathered for a in g]
    kv_cols = 2 * groups * HD

    def kernel(me_ref, lengths_ref, assign_ref, cos_ref, sin_ref, *rest):
        refs, rest = rest[: len(flat)], rest[len(flat) :]
        nested, at = [], 0
        for c in counts:
            nested.append(refs[at : at + c])
            at += c
        k_ref, v_ref = rest[0], rest[1]
        outs = rest[2 : 2 + pieces]
        attend_kernel(
            me_ref, lengths_ref, assign_ref, cos_ref, sin_ref, nested, k_ref, v_ref, outs,
            *rest[2 + pieces :], slots=slots, groups=groups, group_size=heads // groups,
            pieces=pieces, width=width, kv_cols=kv_cols,
        )

    smem = pl.BlockSpec(memory_space=pltpu.SMEM)
    whole = lambda a: pl.BlockSpec(a.shape, lambda i: (0,) * a.ndim)
    cols = heads * HD // pieces
    outs = [jax.ShapeDtypeStruct((slots, cols), BF)] * pieces
    return pl.pallas_call(
        kernel,
        grid=(slots,),
        in_specs=[smem, smem, smem, whole(cosine), whole(sine)]
        + [whole(a) for a in flat]
        + [
            pl.BlockSpec((1, 1, most, channels), lambda i: (i, 0, 0, 0)),
            pl.BlockSpec((1, 1, most, channels), lambda i: (i, 1, 0, 0)),
        ],
        out_specs=[whole(a) for a in outs],
        out_shape=outs,
        scratch_shapes=[
            pltpu.VMEM((heads * 8, HD), F32),
            pltpu.VMEM((8, HD), F32),
            pltpu.VMEM((2 * groups + 1, slots, HD), F32),
            pltpu.VMEM((heads * 8, HD), F32),
        ],
        compiler_params=params(),
    )(me, lengths, assignment, cosine, sine, *flat, cache, cache)


def output_kernel(me_ref, other_ref, assign_ref, *rest, counts, slots, order, row_block, first):
    parts, rest = rest[:counts], rest[counts:]
    if first:
        w_ref, out_ref, lhs = rest
    else:
        before_ref, w_ref, out_ref, lhs = rest
    rows = out_ref.shape[0]
    tile = w_ref.shape[0]
    step = pl.program_id(0)

    @pl.when(step == 0)
    def _():
        out_row = lax.broadcasted_iota(jnp.int32, (rows, rows), 0)
        col = lax.broadcasted_iota(jnp.int32, (rows, rows), 1)
        block = lax.bitwise_xor(lax.shift_right_logical(out_row, log2(row_block)), other_ref[0])
        row = block * row_block + lax.bitwise_and(out_row, row_block - 1)
        named = one_hot(row == assign_ref[...])
        pick = one_hot(slot_of_row(out_row, me_ref[0], slots, order) == col)
        perm = lax.dot_general(named, pick, NT, preferred_element_type=F32).astype(BF)
        at = 0
        total = None
        for part in parts:
            n = part.shape[0]
            term = jnp.dot(perm[:, at : at + n], part[...], preferred_element_type=F32)
            total = term if total is None else total + term
            at += n
        total = total.astype(BF)
        for k in range(lhs.shape[0]):
            lhs[k] = total[:, k * tile : (k + 1) * tile]
        out_ref[...] = jnp.zeros_like(out_ref) if first else before_ref[...]

    out_ref[...] += jnp.dot(lhs[step], w_ref[...], preferred_element_type=F32)


def output(me, other, assignment, parts, w, piece, pieces, slots, order, row_block, before=None):
    rows = sum(a.shape[0] for a in parts)
    depth = w.shape[0] // pieces
    tile = min(1024, depth)
    steps = depth // tile
    smem = pl.BlockSpec(memory_space=pltpu.SMEM)
    whole = lambda a: pl.BlockSpec(a.shape, lambda i: (0,) * a.ndim)
    out = jax.ShapeDtypeStruct((rows, w.shape[1]), F32)
    ins = [me, other, assignment, *parts] + ([] if before is None else [before]) + [w]
    in_specs = [smem, smem, whole(assignment)] + [whole(a) for a in parts]
    if before is not None:
        in_specs.append(whole(before))
    in_specs.append(pl.BlockSpec((tile, w.shape[1]), lambda i: (piece * steps + i, 0)))
    return pl.pallas_call(
        functools.partial(
            output_kernel, counts=len(parts), slots=slots, order=order, row_block=row_block,
            first=before is None,
        ),
        grid=(steps,),
        in_specs=in_specs,
        out_specs=whole(out),
        out_shape=out,
        scratch_shapes=[pltpu.VMEM((steps, rows, tile), BF)],
        compiler_params=params(),
        cost_estimate=pl.CostEstimate(
            flops=2 * rows * depth * w.shape[1],
            bytes_accessed=2 * depth * w.shape[1],
            transcendentals=0,
        ),
    )(*ins)


def angles_of(positions):
    half = HD // 2
    freqs = 500000.0 ** (-(jnp.arange(half, dtype=F32) * 2.0 / HD))
    angles = positions[:, None] * freqs
    cosine, sine = jnp.cos(angles), jnp.sin(angles)
    return jnp.concatenate([cosine, cosine], 1), jnp.concatenate([-sine, sine], 1)


def per_device(residual, norm_gain, w_query, w_keyval, w_out, cache_rows, lengths, assignment):
    n = lax.axis_size("wide")
    slots, most, _, channels = cache_rows.shape
    groups = channels // HD
    heads = w_query.shape[1] // HD
    depth = w_query.shape[0]
    width = depth * n
    row_block = residual.shape[0]
    narrow = lax.axis_size("narrow")
    pieces = 2 if groups % 2 == 0 else 1
    bits = [1 << k for k in range(log2(n))]
    top = bits[2:][::-1]
    orders = [[bits[0], bits[1]] + top, [bits[1], bits[0]] + top][:pieces]

    me = lax.axis_index("wide").astype(jnp.int32)
    me1 = me.reshape(1)
    other1 = lax.axis_index("narrow").astype(jnp.int32).reshape(1)
    named = assignment.reshape(1, -1)
    gathered = lax.all_gather(residual, "narrow", axis=0, tiled=True)
    gain = norm_gain.reshape(1, -1)
    wkv = w_keyval.reshape(depth, 2 * channels)

    state = []
    for p in range(pieces):
        last = p == pieces - 1
        got = project(
            me1, named, gathered, gain, w_query, p, pieces, slots, orders[p], wkv if last else None
        )
        state.append([got[0], got[1], orders[p], False])
        if last:
            state.append([got[2], got[3], orders[p], True])

    for stage in range(len(bits) - 2):
        received = [exchange(send, "wide", order[stage]) for _, send, order, _ in state]
        final = stage == len(bits) - 3
        for k, (keep, _, order, squares) in enumerate(state):
            outs = add_split(keep, received[k], 4 if final else 2, squares)
            state[k] = [outs[0], outs[1:] if final else outs[1], order, squares]
    arrived = []
    for keep, sends, order, _ in state:
        masks = direct_masks(order)
        arrived.append([keep] + [exchange(s, "wide", m) for s, m in zip(sends, masks)])

    cache = jnp.transpose(cache_rows, (0, 2, 1, 3))
    owned = lax.dynamic_slice_in_dim(assignment, me * slots, slots)
    cosine, sine = angles_of(lengths[owned].astype(F32))
    attended = attend(
        me1, lengths, assignment, cosine, sine, arrived, cache, slots, groups, heads, width
    )

    blocks = []
    for p in range(pieces):
        own = attended[p]
        blocks.append(
            [jnp.concatenate([own] + [exchange(own, "wide", m) for m in direct_masks(orders[p])], 0)]
        )
    for stage in reversed(range(len(bits) - 2)):
        for p in range(pieces):
            have = blocks[p][0] if len(blocks[p]) == 1 else jnp.concatenate(blocks[p], 0)
            blocks[p] = blocks[p] + [exchange(have, "wide", orders[p][stage])]
    update = None
    for p in range(pieces):
        update = output(
            me1, other1, named, blocks[p], w_out, p, pieces, slots, orders[p], row_block, update
        )
    bit = narrow // 2
    while bit >= 1:
        half = update.shape[0] // 2
        update = update[:half] + exchange(update[half:], "narrow", bit)
        bit //= 2
    return (residual.astype(F32) + update).astype(BF)


def solution(mesh):
    placed = (
        P("narrow", "wide"),
        P("wide"),
        P("wide", "narrow"),
        P("wide", None, "narrow"),
        P("narrow", "wide"),
        P("wide", None, None, "narrow"),
        P(),
        P(),
    )
    return jax.shard_map(
        per_device, mesh=mesh, in_specs=placed, out_specs=P("narrow", "wide"), check_vma=False
    )
```

time: 303 us -> 94.9 us (0.31)
  waiting for transfers between devices: 169 us -> 16.8 us
  blocking collectives: 45.7 us -> 2.2 us
  starting transfers between devices: 0.09 us -> 34.1 us
  local copies, waits for them, and re-layouts: 41.2 us -> 9.32 us
  Pallas kernels: 0 us -> 30.9 us
  matrix products: 23.3 us -> 0 us
  between operations: 14 us -> 0.21 us
  other arithmetic: 7.9 us -> 1.09 us
    unnamed x4 -> x0, waiting for transfers between devices: 108 us -> none
    all_gather x1 -> x0, waiting for transfers between devices: 54.1 us -> none  [per_device(): lax.all_gather(attended, 'wide', axis=0, tiled=True)]
    psum x1 -> x0, blocking collectives: 43.4 us -> none  [per_device(): squares = lax.psum(jnp.sum(gathered * gathered, axis=1), 'wide')]
    ppermute x0 -> x26, starting transfers between devices: none -> 34.1 us  [exchange(): return lax.ppermute(value, axis, [(i, i ^ bit) for i in range(n)])]
    pallas_call x0 -> x11, Pallas kernels: none -> 30.9 us  [the longest x2 11.4 us: output(): pl.pallas_call(functools.partial(output_kernel, counts=len(parts), slots=...]
    dot_general x16 -> x0, matrix products: 23.3 us -> none  [the longest x1 8.82 us: per_device(): jnp.dot(lax.all_gather(attended, 'wide', axis=0, tiled=True), w_out, pref...]
    ppermute x0 -> x26, waiting for transfers between devices: none -> 16.8 us  [exchange(): return lax.ppermute(value, axis, [(i, i ^ bit) for i in range(n)])]
    slice x13 -> x1, local copies, waits for them, and re-layouts: 15.1 us -> 0.01 us  [per_device(): update = update[:half] + exchange(update[half:], 'narrow', bit)]
  transfers between devices with their start and end apart: 3 -> 26, of which waited for: 3 -> 8; matrix products, arithmetic and copies ran while one was open for 6% -> 9% of each run, Pallas kernels for 0% -> 12%
where the time goes in v1:
time: 94.9 us; the launch traced here: 94.7 us
  starting transfers between devices  34.1 us (36%)
  Pallas kernels  30.9 us (33%)
  waiting for transfers between devices  16.8 us (18%)
  local copies, waits for them, and re-layouts  9.32 us (10%)
  blocking collectives  2.2 us (2%)
  other arithmetic  1.09 us (1%)
    ppermute x26, starting transfers between devices, exchange(): return lax.ppermute(value, axis, [(i, i ^ bit) for i in range(n)])  34.1 us
    ppermute x26, waiting for transfers between devices, exchange(): return lax.ppermute(value, axis, [(i, i ^ bit) for i in range(n)])  16.8 us
    pallas_call x2, Pallas kernels, output(): pl.pallas_call(functools.partial(output_kernel, counts=len(parts), slots=...  11.4 us
    pallas_call x2, Pallas kernels, project(): pl.pallas_call(functools.partial(project_kernel, slots=slots, order=order...  11 us
    pallas_call x1, Pallas kernels, attend(): pl.pallas_call(kernel, grid=(slots,), in_specs=[smem, smem, smem, whole(c...  8.32 us
    unnamed x12, local copies, waits for them, and re-layouts  7.78 us
    all_gather x1, blocking collectives, per_device(): gathered = lax.all_gather(residual, 'narrow', axis=0, tiled=True)  2.2 us
  transfers between devices with their start and end apart: 26, of which 8 were waited for; matrix products, arithmetic and copies ran while one was open for 9% of the time, Pallas kernels for 12%

profile of v1, /device:TPU:0, one launch (start us, length us, event | category | flops | bytes accessed | tf_op | source)
XLA Modules:
  0.0 94.7 jit_solution(11266143630887478978)
XLA Ops:
  0.0 0.7 reshape.27.gain_ref
  0.7 2.2 %all_gather.3.x_ref = bf16[64,1024]{1,0:T(8,128)(2,1)S(1)} all-gather(bf16[32,1024]{1,0:T(8,128)(2,1)} %param.8), channel_id=1, replica_groups=mesh['wide'=16,'narrow'=2] {'narrow'}, dimensions={0}, use_global_device_ids=true | all-gather | bytes 196608 | tf_op jit(solution)/shard_map/all_gather | solution.py:385
  2.9 0.7 copy-done.1
  3.5 5.3 %shard_map.82 = (f32[32,4096]{1,0:T(8,128)S(1)}, bf16[32,4096]{1,0:T(8,128)(2,1)S(1)}) custom-call(s32[1]{0:T(128)} %bitcast.me_ref, s32[1,64]{1,0:T(1,128)S(1)} %bitcast.9, bf16[64,1024]{1,0:T(8,128)(2,1)S(1)} %all_gather.3.x_ref, bf16[1,1024]{1,0:T(2,128)(2,1)S(1)} %reshape.27.gain_ref, bf16[1024,8192]{1,0:T(8,128)(2,1)} %w_ref.3), custom_call_target="tpu_custom_call" | custom-call | flops 1073741824 | bytes 8388608 | tf_op jit(solution)/shard_map/pallas_call | solution.py:114
  8.9 2.9 %collective-permute-start = (bf16[32,4096]{1,0:T(8,128)(2,1)S(1)}, bf16[32,4096]{1,0:T(8,128)(2,1)S(1)}, u32[]{:S(2)}, u32[]{:S(2)}) collective-permute-start(bf16[32,4096]{1,0:T(8,128)(2,1)S(1)} %get-tuple-element.32), channel_id=1, source_target_pairs={{0,2},{2,0},{4,6},{6,4},{8,10},{10,8},{12,14},{14,12},{16,18},{18,... | collective-permute-start | bytes 786440 | tf_op jit(solution)/shard_map/ppermute | solution.py:164
  12.4 5.6 %shard_map.85 = (f32[32,4096]{1,0:T(8,128)S(1)}, bf16[32,4096]{1,0:T(8,128)(2,1)S(1)}, f32[32,1152]{1,0:T(8,128)S(1)}, bf16[32,1280]{1,0:T(8,128)(2,1)S(1)}) custom-call(s32[1]{0:T(128)} %bitcast.me_ref, s32[1,64]{1,0:T(1,128)S(1)} %bitcast.10, bf16[64,1024]{1,0:T(8,128)(2,1)S(1)} %all_gather.3.x_ref, bf16[1,1024]{1,0:T(2,128)(2,1)S(1)} %reshape.27.gain_ref, ...), custom_call_target="tpu_custom_call" | custom-call | flops 1073741824 | bytes 8388608 | tf_op jit(solution)/shard_map/pallas_call | solution.py:114
  18.0 1.6 %collective-permute-start.10 = (bf16[32,1280]{1,0:T(8,128)(2,1)S(1)}, bf16[32,1280]{1,0:T(8,128)(2,1)S(1)}, u32[]{:S(2)}, u32[]{:S(2)}) collective-permute-start(bf16[32,1280]{1,0:T(8,128)(2,1)S(1)} %get-tuple-element.48), channel_id=1, source_target_pairs={{0,4},{2,6},{4,0},{6,2},{8,12},{10,14},{12,8},{14,10},{16,20},{18,... | collective-permute-start | bytes 245768 | tf_op jit(solution)/shard_map/ppermute | solution.py:164
  20.3 1.6 %collective-permute-start.1 = (bf16[16,4096]{1,0:T(8,128)(2,1)S(1)}, bf16[16,4096]{1,0:T(8,128)(2,1)S(1)}, u32[]{:S(2)}, u32[]{:S(2)}) collective-permute-start(bf16[16,4096]{1,0:T(8,128)(2,1)S(1)} %get-tuple-element.34), channel_id=1, source_target_pairs={{0,4},{2,6},{4,0},{6,2},{8,12},{10,14},{12,8},{14,10},{16,20},{18,... | collective-permute-start | bytes 393224 | tf_op jit(solution)/shard_map/ppermute | solution.py:164
  21.9 1.4 %collective-permute-done.10.recv_ref = bf16[32,1280]{1,0:T(8,128)(2,1)S(1)} collective-permute-done((bf16[32,1280]{1,0:T(8,128)(2,1)S(1)}, bf16[32,1280]{1,0:T(8,128)(2,1)S(1)}, u32[]{:S(2)}, u32[]{:S(2)}) %collective-permute-start.10) | collective-permute-done | bytes 81952 | tf_op jit(solution)/shard_map/ppermute | solution.py:164
  24.1 3.3 %collective-permute-done.11.recv_ref = bf16[16,1280]{1,0:T(8,128)(2,1)S(1)} collective-permute-done((bf16[16,1280]{1,0:T(8,128)(2,1)S(1)}, bf16[16,1280]{1,0:T(8,128)(2,1)S(1)}, u32[]{:S(2)}, u32[]{:S(2)}) %collective-permute-start.11) | collective-permute-done | bytes 40992 | tf_op jit(solution)/shard_map/ppermute | solution.py:164
  27.4 1.6 %collective-permute-start.12 = (bf16[4,1280]{1,0:T(4,128)(2,1)S(1)}, bf16[4,1280]{1,0:T(4,128)(2,1)S(1)}, u32[]{:S(2)}, u32[]{:S(2)}) collective-permute-start(bf16[4,1280]{1,0:T(4,128)(2,1)S(1)} %get-tuple-element.52), channel_id=1, source_target_pairs={{0,8},{2,10},{4,12},{6,14},{8,0},{10,2},{12,4},{14,6},{16,24},{18,... | collective-permute-start | bytes 30728 | tf_op jit(solution)/shard_map/ppermute | solution.py:164
  29.0 2.6 %collective-permute-start.13 = (bf16[4,1280]{1,0:T(4,128)(2,1)S(1)}, bf16[4,1280]{1,0:T(4,128)(2,1)S(1)}, u32[]{:S(2)}, u32[]{:S(2)}) collective-permute-start(bf16[4,1280]{1,0:T(4,128)(2,1)S(1)} %get-tuple-element.53), channel_id=1, source_target_pairs={{0,16},{2,18},{4,20},{6,22},{8,24},{10,26},{12,28},{14,30},{16,0},... | collective-permute-start | bytes 30728 | tf_op jit(solution)/shard_map/ppermute | solution.py:164
  32.3 1.0 %collective-permute-start.2 = (bf16[4,4096]{1,0:T(4,128)(2,1)S(1)}, bf16[4,4096]{1,0:T(4,128)(2,1)S(1)}, u32[]{:S(2)}, u32[]{:S(2)}) collective-permute-start(bf16[4,4096]{1,0:T(4,128)(2,1)S(1)} %get-tuple-element.36), channel_id=1, source_target_pairs={{0,8},{2,10},{4,12},{6,14},{8,0},{10,2},{12,4},{14,6},{16,24},{18,... | collective-permute-start | bytes 98312 | tf_op jit(solution)/shard_map/ppermute | solution.py:164
  33.4 3.5 %collective-permute-done.6.recv_ref = bf16[16,4096]{1,0:T(8,128)(2,1)S(1)} collective-permute-done((bf16[16,4096]{1,0:T(8,128)(2,1)S(1)}, bf16[16,4096]{1,0:T(8,128)(2,1)S(1)}, u32[]{:S(2)}, u32[]{:S(2)}) %collective-permute-start.6) | collective-permute-done | bytes 131104 | tf_op jit(solution)/shard_map/ppermute | solution.py:164
  36.9 1.7 %collective-permute-start.3 = (bf16[4,4096]{1,0:T(4,128)(2,1)S(1)}, bf16[4,4096]{1,0:T(4,128)(2,1)S(1)}, u32[]{:S(2)}, u32[]{:S(2)}) collective-permute-start(bf16[4,4096]{1,0:T(4,128)(2,1)S(1)} %get-tuple-element.37), channel_id=1, source_target_pairs={{0,16},{2,18},{4,20},{6,22},{8,24},{10,26},{12,28},{14,30},{16,0},... | collective-permute-start | bytes 98312 | tf_op jit(solution)/shard_map/ppermute | solution.py:164
  38.7 2.0 %collective-permute-start.4 = (bf16[4,4096]{1,0:T(4,128)(2,1)S(1)}, bf16[4,4096]{1,0:T(4,128)(2,1)S(1)}, u32[]{:S(2)}, u32[]{:S(2)}) collective-permute-start(bf16[4,4096]{1,0:T(4,128)(2,1)S(1)} %get-tuple-element.38), channel_id=1, source_target_pairs={{0,24},{2,26},{4,28},{6,30},{8,16},{10,18},{12,20},{14,22},{16,8},... | collective-permute-start | bytes 98312 | tf_op jit(solution)/shard_map/ppermute | solution.py:164
  41.3 1.8 %collective-permute-start.8 = (bf16[4,4096]{1,0:T(4,128)(2,1)S(1)}, bf16[4,4096]{1,0:T(4,128)(2,1)S(1)}, u32[]{:S(2)}, u32[]{:S(2)}) collective-permute-start(bf16[4,4096]{1,0:T(4,128)(2,1)S(1)} %get-tuple-element.45), channel_id=1, source_target_pairs={{0,16},{2,18},{4,20},{6,22},{8,24},{10,26},{12,28},{14,30},{16,0},... | collective-permute-start | bytes 98312 | tf_op jit(solution)/shard_map/ppermute | solution.py:164
  43.1 1.9 %collective-permute-start.9 = (bf16[4,4096]{1,0:T(4,128)(2,1)S(1)}, bf16[4,4096]{1,0:T(4,128)(2,1)S(1)}, u32[]{:S(2)}, u32[]{:S(2)}) collective-permute-start(bf16[4,4096]{1,0:T(4,128)(2,1)S(1)} %get-tuple-element.46), channel_id=1, source_target_pairs={{0,24},{2,26},{4,28},{6,30},{8,16},{10,18},{12,20},{14,22},{16,8},... | collective-permute-start | bytes 98312 | tf_op jit(solution)/shard_map/ppermute | solution.py:164
  45.1 6.5 %copy.13 = bf16[4,768,2,512]{3,1,2,0:T(8,128)(2,1)} copy(bf16[4,768,2,512]{3,2,1,0:T(2,128)(2,1)} %param.13) | data formatting | bytes 12582912 | tf_op args[5]
  51.7 8.3 %shard_map.90 = (bf16[4,4096]{1,0:T(4,128)(2,1)S(1)}, bf16[4,4096]{1,0:T(4,128)(2,1)S(1)}) custom-call(s32[1]{0:T(128)} %bitcast.me_ref, s32[64]{0:T(128)S(1)} %copy-done, s32[64]{0:T(128)S(1)} %copy-done.2, f32[4,128]{1,0:T(4,128)S(1)} %get-tuple-element.60.cos_ref, f32[4,128]{1,0:T(4,128)S(1)} %get-tuple-element.61.sin_ref, ...), custom_call_target="tpu_custom_call" | custom-call | tf_op jit(solution)/shard_map/pallas_call | solution.py:272
  60.1 2.0 %collective-permute-start.22 = (bf16[4,4096]{1,0:T(4,128)(2,1)S(1)}, bf16[4,4096]{1,0:T(4,128)(2,1)S(1)}, u32[]{:S(2)}, u32[]{:S(2)}) collective-permute-start(bf16[4,4096]{1,0:T(4,128)(2,1)S(1)} %get-tuple-element.56), channel_id=1, source_target_pairs={{0,24},{2,26},{4,28},{6,30},{8,16},{10,18},{12,20},{14,22},{16,8},... | collective-permute-start | bytes 98312 | tf_op jit(solution)/shard_map/ppermute | solution.py:164
  62.0 2.5 %collective-permute-start.20 = (bf16[4,4096]{1,0:T(4,128)(2,1)S(1)}, bf16[4,4096]{1,0:T(4,128)(2,1)S(1)}, u32[]{:S(2)}, u32[]{:S(2)}) collective-permute-start(bf16[4,4096]{1,0:T(4,128)(2,1)S(1)} %get-tuple-element.56), channel_id=1, source_target_pairs={{0,8},{2,10},{4,12},{6,14},{8,0},{10,2},{12,4},{14,6},{16,24},{18,... | collective-permute-start | bytes 98312 | tf_op jit(solution)/shard_map/ppermute | solution.py:164
  64.5 1.9 %collective-permute-start.17 = (bf16[4,4096]{1,0:T(4,128)(2,1)S(1)}, bf16[4,4096]{1,0:T(4,128)(2,1)S(1)}, u32[]{:S(2)}, u32[]{:S(2)}) collective-permute-start(bf16[4,4096]{1,0:T(4,128)(2,1)S(1)} %get-tuple-element.55), channel_id=1, source_target_pairs={{0,24},{2,26},{4,28},{6,30},{8,16},{10,18},{12,20},{14,22},{16,8},... | collective-permute-start | bytes 98312 | tf_op jit(solution)/shard_map/ppermute | solution.py:164
  66.4 2.5 %collective-permute-start.15 = (bf16[4,4096]{1,0:T(4,128)(2,1)S(1)}, bf16[4,4096]{1,0:T(4,128)(2,1)S(1)}, u32[]{:S(2)}, u32[]{:S(2)}) collective-permute-start(bf16[4,4096]{1,0:T(4,128)(2,1)S(1)} %get-tuple-element.55), channel_id=1, source_target_pairs={{0,8},{2,10},{4,12},{6,14},{8,0},{10,2},{12,4},{14,6},{16,24},{18,... | collective-permute-start | bytes 98312 | tf_op jit(solution)/shard_map/ppermute | solution.py:164
  69.0 1.7 %collective-permute-start.23 = (bf16[16,4096]{1,0:T(8,128)(2,1)S(1)}, bf16[16,4096]{1,0:T(8,128)(2,1)S(1)}, u32[]{:S(2)}, u32[]{:S(2)}) collective-permute-start(bf16[16,4096]{1,0:T(8,128)(2,1)S(1)} %pad_maximum_fusion.1.rest_0_), channel_id=1, source_target_pairs={{0,4},{2,6},{4,0},{6,2},{8,12},{10,14},{12,8},{14,10},{16,20},{18,... | collective-permute-start | bytes 393224 | tf_op jit(solution)/shard_map/ppermute | solution.py:164
  71.9 2.7 %collective-permute-done.23.rest_1_ = bf16[16,4096]{1,0:T(8,128)(2,1)S(1)} collective-permute-done((bf16[16,4096]{1,0:T(8,128)(2,1)S(1)}, bf16[16,4096]{1,0:T(8,128)(2,1)S(1)}, u32[]{:S(2)}, u32[]{:S(2)}) %collective-permute-start.23) | collective-permute-done | bytes 131104 | tf_op jit(solution)/shard_map/ppermute | solution.py:164
  75.3 1.1 %collective-permute-done.18.rest_1_ = bf16[16,4096]{1,0:T(8,128)(2,1)S(1)} collective-permute-done((bf16[16,4096]{1,0:T(8,128)(2,1)S(1)}, bf16[16,4096]{1,0:T(8,128)(2,1)S(1)}, u32[]{:S(2)}, u32[]{:S(2)}) %collective-permute-start.18) | collective-permute-done | bytes 131104 | tf_op jit(solution)/shard_map/ppermute | solution.py:164
  76.4 1.7 %collective-permute-start.19 = (bf16[32,4096]{1,0:T(8,128)(2,1)S(1)}, bf16[32,4096]{1,0:T(8,128)(2,1)S(1)}, u32[]{:S(2)}, u32[]{:S(2)}) collective-permute-start(bf16[32,4096]{1,0:T(8,128)(2,1)S(1)} %concatenate.23), channel_id=1, source_target_pairs={{0,4},{2,6},{4,0},{6,2},{8,12},{10,14},{12,8},{14,10},{16,20},{18,... | collective-permute-start | bytes 786440 | tf_op jit(solution)/shard_map/ppermute | solution.py:164
  78.2 2.9 %collective-permute-done.24.rest_2_ = bf16[32,4096]{1,0:T(8,128)(2,1)S(1)} collective-permute-done((bf16[32,4096]{1,0:T(8,128)(2,1)S(1)}, bf16[32,4096]{1,0:T(8,128)(2,1)S(1)}, u32[]{:S(2)}, u32[]{:S(2)}) %collective-permute-start.24) | collective-permute-done | bytes 262176 | tf_op jit(solution)/shard_map/ppermute | solution.py:164
  81.1 5.7 %shard_map.91.rest_3_ = f32[64,1024]{1,0:T(8,128)S(1)} custom-call(s32[1]{0:T(128)} %bitcast.me_ref, s32[1]{0:T(128)} %bitcast.1.other_ref, s32[1,64]{1,0:T(1,128)S(1)} %bitcast.11, bf16[16,4096]{1,0:T(8,128)(2,1)S(1)} %pad_maximum_fusion.1.rest_0_, bf16[16,4096]{1,0:T(8,128)(2,1)S(1)} %collective-permute-done.23.rest_1_, ...), custom_call_target="tpu_custom_call" | custom-call | flops 536870912 | bytes 8388608 | tf_op jit(solution)/shard_map/pallas_call | solution.py:340
  86.8 5.7 %shard_map.92 = f32[64,1024]{1,0:T(8,128)S(1)} custom-call(s32[1]{0:T(128)} %bitcast.me_ref, s32[1]{0:T(128)} %bitcast.1.other_ref, s32[1,64]{1,0:T(1,128)S(1)} %bitcast.12, bf16[16,4096]{1,0:T(8,128)(2,1)S(1)} %pad_maximum_fusion.rest_0_, bf16[16,4096]{1,0:T(8,128)(2,1)S(1)} %collective-permute-done.18.rest_1_, ...), custom_call_target="tpu_custom_call" | custom-call | flops 536870912 | bytes 8388608 | tf_op jit(solution)/shard_map/pallas_call | solution.py:340
  92.7 1.3 %collective-permute-done.25 = f32[32,1024]{1,0:T(8,128)S(1)} collective-permute-done((f32[32,1024]{1,0:T(8,128)S(1)}, f32[32,1024]{1,0:T(8,128)S(1)}, u32[]{:S(2)}, u32[]{:S(2)}) %collective-permute-start.25) | collective-permute-done | bytes 131104 | tf_op jit(solution)/shard_map/ppermute | solution.py:164
  (58 shorter events, 6.3 us)
Async XLA Ops:
  2.9 0.7 copy-start.1
  3.5 8.3 %copy-start.3 = (bf16[1024,2,512]{2,1,0:T(2,128)(2,1)S(1)}, bf16[1024,2,512]{2,1,0:T(2,128)(2,1)}, u32[]{:S(2)}) copy-start(bf16[1024,2,512]{2,1,0:T(2,128)(2,1)} %param.11) | copy-start | bytes 6291460
  8.9 11.3 %collective-permute-start = (bf16[32,4096]{1,0:T(8,128)(2,1)S(1)}, bf16[32,4096]{1,0:T(8,128)(2,1)S(1)}, u32[]{:S(2)}, u32[]{:S(2)}) collective-permute-start(bf16[32,4096]{1,0:T(8,128)(2,1)S(1)} %get-tuple-element.32), channel_id=1, source_target_pairs={{0,2},{2,0},{4,6},{6,4},{8,10},{10,8},{12,14},{14,12},{16,18},{18,... | collective-permute-start | bytes 786440 | tf_op jit(solution)/shard_map/ppermute | solution.py:164
  12.4 7.8 %copy-start.2 = (s32[64]{0:T(128)S(1)}, s32[64]{0:T(128)}, u32[]{:S(2)}) copy-start(s32[64]{0:T(128)} %assign_ref.1) | copy-start | bytes 772
  12.4 11.0 %copy-start = (s32[64]{0:T(128)S(1)}, s32[64]{0:T(128)}, u32[]{:S(2)}) copy-start(s32[64]{0:T(128)} %lengths_ref.1) | copy-start | bytes 772
  18.0 5.2 %collective-permute-start.10 = (bf16[32,1280]{1,0:T(8,128)(2,1)S(1)}, bf16[32,1280]{1,0:T(8,128)(2,1)S(1)}, u32[]{:S(2)}, u32[]{:S(2)}) collective-permute-start(bf16[32,1280]{1,0:T(8,128)(2,1)S(1)} %get-tuple-element.48), channel_id=1, source_target_pairs={{0,4},{2,6},{4,0},{6,2},{8,12},{10,14},{12,8},{14,10},{16,20},{18,... | collective-permute-start | bytes 245768 | tf_op jit(solution)/shard_map/ppermute | solution.py:164
  19.6 12.2 %collective-permute-start.5 = (bf16[32,4096]{1,0:T(8,128)(2,1)S(1)}, bf16[32,4096]{1,0:T(8,128)(2,1)S(1)}, u32[]{:S(2)}, u32[]{:S(2)}) collective-permute-start(bf16[32,4096]{1,0:T(8,128)(2,1)S(1)} %get-tuple-element.40), channel_id=1, source_target_pairs={{0,4},{2,6},{4,0},{6,2},{8,12},{10,14},{12,8},{14,10},{16,20},{18,... | collective-permute-start | bytes 786440 | tf_op jit(solution)/shard_map/ppermute | solution.py:164
  20.3 12.0 %collective-permute-start.1 = (bf16[16,4096]{1,0:T(8,128)(2,1)S(1)}, bf16[16,4096]{1,0:T(8,128)(2,1)S(1)}, u32[]{:S(2)}, u32[]{:S(2)}) collective-permute-start(bf16[16,4096]{1,0:T(8,128)(2,1)S(1)} %get-tuple-element.34), channel_id=1, source_target_pairs={{0,4},{2,6},{4,0},{6,2},{8,12},{10,14},{12,8},{14,10},{16,20},{18,... | collective-permute-start | bytes 393224 | tf_op jit(solution)/shard_map/ppermute | solution.py:164
  23.3 4.1 %collective-permute-start.11 = (bf16[16,1280]{1,0:T(8,128)(2,1)S(1)}, bf16[16,1280]{1,0:T(8,128)(2,1)S(1)}, u32[]{:S(2)}, u32[]{:S(2)}) collective-permute-start(bf16[16,1280]{1,0:T(8,128)(2,1)S(1)} %get-tuple-element.50), channel_id=1, source_target_pairs={{0,2},{2,0},{4,6},{6,4},{8,10},{10,8},{12,14},{14,12},{16,18},{18,... | collective-permute-start | bytes 122888 | tf_op jit(solution)/shard_map/ppermute | solution.py:164
  27.4 11.3 %collective-permute-start.12 = (bf16[4,1280]{1,0:T(4,128)(2,1)S(1)}, bf16[4,1280]{1,0:T(4,128)(2,1)S(1)}, u32[]{:S(2)}, u32[]{:S(2)}) collective-permute-start(bf16[4,1280]{1,0:T(4,128)(2,1)S(1)} %get-tuple-element.52), channel_id=1, source_target_pairs={{0,8},{2,10},{4,12},{6,14},{8,0},{10,2},{12,4},{14,6},{16,24},{18,... | collective-permute-start | bytes 30728 | tf_op jit(solution)/shard_map/ppermute | solution.py:164
  29.0 11.6 %collective-permute-start.13 = (bf16[4,1280]{1,0:T(4,128)(2,1)S(1)}, bf16[4,1280]{1,0:T(4,128)(2,1)S(1)}, u32[]{:S(2)}, u32[]{:S(2)}) collective-permute-start(bf16[4,1280]{1,0:T(4,128)(2,1)S(1)} %get-tuple-element.53), channel_id=1, source_target_pairs={{0,16},{2,18},{4,20},{6,22},{8,24},{10,26},{12,28},{14,30},{16,0},... | collective-permute-start | bytes 30728 | tf_op jit(solution)/shard_map/ppermute | solution.py:164
  31.6 9.7 %collective-permute-start.14 = (bf16[4,1280]{1,0:T(4,128)(2,1)S(1)}, bf16[4,1280]{1,0:T(4,128)(2,1)S(1)}, u32[]{:S(2)}, u32[]{:S(2)}) collective-permute-start(bf16[4,1280]{1,0:T(4,128)(2,1)S(1)} %get-tuple-element.54), channel_id=1, source_target_pairs={{0,24},{2,26},{4,28},{6,30},{8,16},{10,18},{12,20},{14,22},{16,8},... | collective-permute-start | bytes 30728 | tf_op jit(solution)/shard_map/ppermute | solution.py:164
  31.9 5.0 %collective-permute-start.6 = (bf16[16,4096]{1,0:T(8,128)(2,1)S(1)}, bf16[16,4096]{1,0:T(8,128)(2,1)S(1)}, u32[]{:S(2)}, u32[]{:S(2)}) collective-permute-start(bf16[16,4096]{1,0:T(8,128)(2,1)S(1)} %get-tuple-element.42), channel_id=1, source_target_pairs={{0,2},{2,0},{4,6},{6,4},{8,10},{10,8},{12,14},{14,12},{16,18},{18,... | collective-permute-start | bytes 393224 | tf_op jit(solution)/shard_map/ppermute | solution.py:164
  32.3 10.8 %collective-permute-start.2 = (bf16[4,4096]{1,0:T(4,128)(2,1)S(1)}, bf16[4,4096]{1,0:T(4,128)(2,1)S(1)}, u32[]{:S(2)}, u32[]{:S(2)}) collective-permute-start(bf16[4,4096]{1,0:T(4,128)(2,1)S(1)} %get-tuple-element.36), channel_id=1, source_target_pairs={{0,8},{2,10},{4,12},{6,14},{8,0},{10,2},{12,4},{14,6},{16,24},{18,... | collective-permute-start | bytes 98312 | tf_op jit(solution)/shard_map/ppermute | solution.py:164
  36.9 14.8 %collective-permute-start.3 = (bf16[4,4096]{1,0:T(4,128)(2,1)S(1)}, bf16[4,4096]{1,0:T(4,128)(2,1)S(1)}, u32[]{:S(2)}, u32[]{:S(2)}) collective-permute-start(bf16[4,4096]{1,0:T(4,128)(2,1)S(1)} %get-tuple-element.37), channel_id=1, source_target_pairs={{0,16},{2,18},{4,20},{6,22},{8,24},{10,26},{12,28},{14,30},{16,0},... | collective-permute-start | bytes 98312 | tf_op jit(solution)/shard_map/ppermute | solution.py:164
  38.7 13.0 %collective-permute-start.4 = (bf16[4,4096]{1,0:T(4,128)(2,1)S(1)}, bf16[4,4096]{1,0:T(4,128)(2,1)S(1)}, u32[]{:S(2)}, u32[]{:S(2)}) collective-permute-start(bf16[4,4096]{1,0:T(4,128)(2,1)S(1)} %get-tuple-element.38), channel_id=1, source_target_pairs={{0,24},{2,26},{4,28},{6,30},{8,16},{10,18},{12,20},{14,22},{16,8},... | collective-permute-start | bytes 98312 | tf_op jit(solution)/shard_map/ppermute | solution.py:164
  40.7 11.0 %collective-permute-start.7 = (bf16[4,4096]{1,0:T(4,128)(2,1)S(1)}, bf16[4,4096]{1,0:T(4,128)(2,1)S(1)}, u32[]{:S(2)}, u32[]{:S(2)}) collective-permute-start(bf16[4,4096]{1,0:T(4,128)(2,1)S(1)} %get-tuple-element.44), channel_id=1, source_target_pairs={{0,8},{2,10},{4,12},{6,14},{8,0},{10,2},{12,4},{14,6},{16,24},{18,... | collective-permute-start | bytes 98312 | tf_op jit(solution)/shard_map/ppermute | solution.py:164
  41.3 10.4 %collective-permute-start.8 = (bf16[4,4096]{1,0:T(4,128)(2,1)S(1)}, bf16[4,4096]{1,0:T(4,128)(2,1)S(1)}, u32[]{:S(2)}, u32[]{:S(2)}) collective-permute-start(bf16[4,4096]{1,0:T(4,128)(2,1)S(1)} %get-tuple-element.45), channel_id=1, source_target_pairs={{0,16},{2,18},{4,20},{6,22},{8,24},{10,26},{12,28},{14,30},{16,0},... | collective-permute-start | bytes 98312 | tf_op jit(solution)/shard_map/ppermute | solution.py:164
  43.1 8.6 %collective-permute-start.9 = (bf16[4,4096]{1,0:T(4,128)(2,1)S(1)}, bf16[4,4096]{1,0:T(4,128)(2,1)S(1)}, u32[]{:S(2)}, u32[]{:S(2)}) collective-permute-start(bf16[4,4096]{1,0:T(4,128)(2,1)S(1)} %get-tuple-element.46), channel_id=1, source_target_pairs={{0,24},{2,26},{4,28},{6,30},{8,16},{10,18},{12,20},{14,22},{16,8},... | collective-permute-start | bytes 98312 | tf_op jit(solution)/shard_map/ppermute | solution.py:164
  60.1 6.4 %collective-permute-start.22 = (bf16[4,4096]{1,0:T(4,128)(2,1)S(1)}, bf16[4,4096]{1,0:T(4,128)(2,1)S(1)}, u32[]{:S(2)}, u32[]{:S(2)}) collective-permute-start(bf16[4,4096]{1,0:T(4,128)(2,1)S(1)} %get-tuple-element.56), channel_id=1, source_target_pairs={{0,24},{2,26},{4,28},{6,30},{8,16},{10,18},{12,20},{14,22},{16,8},... | collective-permute-start | bytes 98312 | tf_op jit(solution)/shard_map/ppermute | solution.py:164
  62.0 6.9 %collective-permute-start.21 = (bf16[4,4096]{1,0:T(4,128)(2,1)S(1)}, bf16[4,4096]{1,0:T(4,128)(2,1)S(1)}, u32[]{:S(2)}, u32[]{:S(2)}) collective-permute-start(bf16[4,4096]{1,0:T(4,128)(2,1)S(1)} %get-tuple-element.56), channel_id=1, source_target_pairs={{0,16},{2,18},{4,20},{6,22},{8,24},{10,26},{12,28},{14,30},{16,0},... | collective-permute-start | bytes 98312 | tf_op jit(solution)/shard_map/ppermute | solution.py:164
  62.0 6.9 %collective-permute-start.20 = (bf16[4,4096]{1,0:T(4,128)(2,1)S(1)}, bf16[4,4096]{1,0:T(4,128)(2,1)S(1)}, u32[]{:S(2)}, u32[]{:S(2)}) collective-permute-start(bf16[4,4096]{1,0:T(4,128)(2,1)S(1)} %get-tuple-element.56), channel_id=1, source_target_pairs={{0,8},{2,10},{4,12},{6,14},{8,0},{10,2},{12,4},{14,6},{16,24},{18,... | collective-permute-start | bytes 98312 | tf_op jit(solution)/shard_map/ppermute | solution.py:164
  64.5 6.2 %collective-permute-start.17 = (bf16[4,4096]{1,0:T(4,128)(2,1)S(1)}, bf16[4,4096]{1,0:T(4,128)(2,1)S(1)}, u32[]{:S(2)}, u32[]{:S(2)}) collective-permute-start(bf16[4,4096]{1,0:T(4,128)(2,1)S(1)} %get-tuple-element.55), channel_id=1, source_target_pairs={{0,24},{2,26},{4,28},{6,30},{8,16},{10,18},{12,20},{14,22},{16,8},... | collective-permute-start | bytes 98312 | tf_op jit(solution)/shard_map/ppermute | solution.py:164
  66.4 4.8 %collective-permute-start.16 = (bf16[4,4096]{1,0:T(4,128)(2,1)S(1)}, bf16[4,4096]{1,0:T(4,128)(2,1)S(1)}, u32[]{:S(2)}, u32[]{:S(2)}) collective-permute-start(bf16[4,4096]{1,0:T(4,128)(2,1)S(1)} %get-tuple-element.55), channel_id=1, source_target_pairs={{0,16},{2,18},{4,20},{6,22},{8,24},{10,26},{12,28},{14,30},{16,0},... | collective-permute-start | bytes 98312 | tf_op jit(solution)/shard_map/ppermute | solution.py:164
  66.4 4.8 %collective-permute-start.15 = (bf16[4,4096]{1,0:T(4,128)(2,1)S(1)}, bf16[4,4096]{1,0:T(4,128)(2,1)S(1)}, u32[]{:S(2)}, u32[]{:S(2)}) collective-permute-start(bf16[4,4096]{1,0:T(4,128)(2,1)S(1)} %get-tuple-element.55), channel_id=1, source_target_pairs={{0,8},{2,10},{4,12},{6,14},{8,0},{10,2},{12,4},{14,6},{16,24},{18,... | collective-permute-start | bytes 98312 | tf_op jit(solution)/shard_map/ppermute | solution.py:164
  69.0 5.6 %collective-permute-start.23 = (bf16[16,4096]{1,0:T(8,128)(2,1)S(1)}, bf16[16,4096]{1,0:T(8,128)(2,1)S(1)}, u32[]{:S(2)}, u32[]{:S(2)}) collective-permute-start(bf16[16,4096]{1,0:T(8,128)(2,1)S(1)} %pad_maximum_fusion.1.rest_0_), channel_id=1, source_target_pairs={{0,4},{2,6},{4,0},{6,2},{8,12},{10,14},{12,8},{14,10},{16,20},{18,... | collective-permute-start | bytes 393224 | tf_op jit(solution)/shard_map/ppermute | solution.py:164
  71.3 5.0 %collective-permute-start.18 = (bf16[16,4096]{1,0:T(8,128)(2,1)S(1)}, bf16[16,4096]{1,0:T(8,128)(2,1)S(1)}, u32[]{:S(2)}, u32[]{:S(2)}) collective-permute-start(bf16[16,4096]{1,0:T(8,128)(2,1)S(1)} %pad_maximum_fusion.rest_0_), channel_id=1, source_target_pairs={{0,2},{2,0},{4,6},{6,4},{8,10},{10,8},{12,14},{14,12},{16,18},{18,... | collective-permute-start | bytes 393224 | tf_op jit(solution)/shard_map/ppermute | solution.py:164
  74.7 6.4 %collective-permute-start.24 = (bf16[32,4096]{1,0:T(8,128)(2,1)S(1)}, bf16[32,4096]{1,0:T(8,128)(2,1)S(1)}, u32[]{:S(2)}, u32[]{:S(2)}) collective-permute-start(bf16[32,4096]{1,0:T(8,128)(2,1)S(1)} %concatenate.25), channel_id=1, source_target_pairs={{0,2},{2,0},{4,6},{6,4},{8,10},{10,8},{12,14},{14,12},{16,18},{18,... | collective-permute-start | bytes 786440 | tf_op jit(solution)/shard_map/ppermute | solution.py:164
  76.4 10.4 %collective-permute-start.19 = (bf16[32,4096]{1,0:T(8,128)(2,1)S(1)}, bf16[32,4096]{1,0:T(8,128)(2,1)S(1)}, u32[]{:S(2)}, u32[]{:S(2)}) collective-permute-start(bf16[32,4096]{1,0:T(8,128)(2,1)S(1)} %concatenate.23), channel_id=1, source_target_pairs={{0,4},{2,6},{4,0},{6,2},{8,12},{10,14},{12,8},{14,10},{16,20},{18,... | collective-permute-start | bytes 786440 | tf_op jit(solution)/shard_map/ppermute | solution.py:164
  86.8 7.2 %copy-start.4 = (bf16[32,1024]{1,0:T(8,128)(2,1)S(1)}, bf16[32,1024]{1,0:T(8,128)(2,1)}, u32[]{:S(2)}) copy-start(bf16[32,1024]{1,0:T(8,128)(2,1)} %param.8) | copy-start | bytes 196612
  92.6 1.4 %collective-permute-start.25 = (f32[32,1024]{1,0:T(8,128)S(1)}, f32[32,1024]{1,0:T(8,128)S(1)}, u32[]{:S(2)}, u32[]{:S(2)}) collective-permute-start(f32[32,1024]{1,0:T(8,128)S(1)} %slice.11), channel_id=1, source_target_pairs={{0,1},{1,0},{2,3},{3,2},{4,5},{5,4},{6,7},{7,6},{8,9},{9,8},{10,11... | collective-permute-start | bytes 393224 | tf_op jit(solution)/shard_map/ppermute | solution.py:164
